TPU v7x, 32 devices: a whole 2x2x4 slice. The times are simulated.
32 devices in a mesh: dp: 32 (over z, y, x, core).
Axes of the slice: x: 2, y: 2, z: 4, core: 2. Of those that a mesh axis runs over, the one named last changes fastest.
Arguments:
- images: bfloat16 [8192, 1152], P('dp'), may hold values from -6 to 6
- texts: bfloat16 [8192, 1152], P('dp'), may hold values from -6 to 6
- plan: int32 [2, 32], replicated, may hold values from 0 to 31, as said below
Outputs:
- row_loss: float32 [8192], P('dp')
- image_grad: bfloat16 [8192, 1152], P('dp')
- text_grad: bfloat16 [8192, 1152], P('dp')
Inputs may be any that keep to these rules, and one draw needn't show every extreme that they name: `plan`: in round r every block's partner is its index XOR a mask m_r common to all blocks, whose highest set bit is bit log2(32) - 1 - r; so partners pair up mutually, differ from the block itself, and differ between rounds.
All inputs are finite; a program needn't handle non-finite values.
Results may differ from a plain program's by a relative error of at most 0.0052.
Values may be sent and summed in bfloat16 or wider, within the bound.
A program may use at most 64 MiB of HBM per device.

v0:
```python
import functools

import jax
import jax.numpy as jnp
from jax import lax
from jax.experimental import pallas as pl
from jax.experimental.pallas import tpu as pltpu
from jax.sharding import PartitionSpec as P

MESH = pl.DeviceIdType.MESH
ROUNDS = 2
TEMPER = 2.0
OFFSET = -1.0
KERNEL_DEVICES = 32
CORE, FIRST, SECOND, NEAR, FAR = 1, 2, 4, 8, 16
PARTS = 4
CHUNKS = 2 * PARTS
HOP_BITS = 2


def flip(index, bit):
    return index + bit - 2 * bit * ((index // bit) % 2)


def pick(own, other, taken):
    mixed = own.astype(jnp.float32) * (1.0 - taken) + other.astype(jnp.float32) * taken
    return mixed.astype(jnp.bfloat16)


def loss_and_slope(t):
    e = jnp.exp(-jnp.abs(t))
    r = 1.0 / (1.0 + e)
    return jnp.maximum(t, 0.0) + jnp.log1p(e), jnp.where(t >= 0.0, r, e * r)


def logits(img, txt, scale):
    dims = (((1,), (1,)), ((), ()))
    return lax.dot_general(img, txt, dims, preferred_element_type=jnp.float32) * scale + OFFSET


def over_rows(g, img):
    return lax.dot_general(g, img, (((0,), (0,)), ((), ())), preferred_element_type=jnp.float32)


def kernel(
    far_bits, scale, taken, img, txt, loss_out, igrad_out, tgrad_out,
    a_recv, b_send, b_recv, c_send, c_recv, d_recv, other, losses, igrad, tgrad,
    a_sems, b_sems, c_sems, d_sems,
):
    me = lax.axis_index("dp")
    core, first, second, near = (flip(me, bit) for bit in (CORE, FIRST, SECOND, NEAR))
    far = me
    for bit in far_bits:
        far = flip(far, bit)
    rows = img.shape[0]
    part = rows // PARTS

    barrier = pltpu.get_barrier_semaphore()
    for device in (core, first, second, near, far):
        pl.semaphore_signal(barrier, inc=1, device_id=(device,), device_id_type=MESH)
    pl.semaphore_wait(barrier, 5)

    def copy(src, dst, sems, place, device):
        return pltpu.make_async_remote_copy(
            src_ref=src, dst_ref=dst, send_sem=sems.at[(0, *place)], recv_sem=sems.at[(1, *place)],
            device_id=(device,), device_id_type=MESH,
        )

    def own(j):
        return (txt if j < PARTS else img).at[pl.ds((j % PARTS) * part, part)]

    order = [(first, second) if j % 2 == 0 else (second, first) for j in range(CHUNKS)]
    bits = [(1, 2) if j % 2 == 0 else (2, 1) for j in range(CHUNKS)]
    a = [copy(own(j), a_recv.at[j], a_sems, (j,), order[j][0]) for j in range(CHUNKS)]
    b = [copy(b_send.at[j], b_recv.at[j], b_sems, (j,), order[j][1]) for j in range(CHUNKS)]
    c = [
        [copy(c_send.at[j, rr], c_recv.at[j, rr], c_sems, (j, rr), (far, near)[rr]) for rr in range(ROUNDS)]
        for j in range(CHUNKS)
    ]
    d = [copy(c_recv.at[j], d_recv.at[j], d_sems, (j,), core) for j in range(CHUNKS)]

    def diagonal():
        z = logits(img[...], txt[...], scale)
        shape = (rows, rows)
        same = lax.broadcasted_iota(jnp.int32, shape, 0) == lax.broadcasted_iota(jnp.int32, shape, 1)
        loss, slope = loss_and_slope(jnp.where(same, -z, z))
        losses[...] = loss
        g = jnp.where(same, -slope, slope).astype(jnp.bfloat16)
        igrad[...] = jnp.dot(g, txt[...], preferred_element_type=jnp.float32)
        tgrad[...] = over_rows(g, img[...])

    a[0].start()
    a[1].start()
    for j in range(CHUNKS + 1):
        if j < CHUNKS:
            a[j].wait_recv()
            for rr in range(ROUNDS):
                b_send[j, rr] = pick(own(j)[...], a_recv[j], taken[rr, bits[j][0]])
            b[j].start()
            if j + 2 < CHUNKS:
                a[j + 2].start()
        if j >= 1:
            b[j - 1].wait_recv()
            for rr in range(ROUNDS):
                c_send[j - 1, rr] = pick(b_send[j - 1, rr], b_recv[j - 1, rr], taken[rr, bits[j - 1][1]])
                c[j - 1][rr].start()
        if j == 3:
            diagonal()

    def finish(j):
        d[j].wait_recv()
        for rr in range(ROUNDS):
            arrived = pick(c_recv[j, rr], d_recv[j, rr], taken[rr, 0])
            if j < PARTS:
                other[rr, pl.ds(j * part, part)] = arrived
            else:
                _, slope = loss_and_slope(logits(arrived, txt[...], scale))
                tgrad[...] += over_rows(slope.astype(jnp.bfloat16), arrived)
        if j == PARTS - 1:
            for rr in range(ROUNDS):
                loss, slope = loss_and_slope(logits(img[...], other[rr], scale))
                losses[...] += loss
                igrad[...] += jnp.dot(slope.astype(jnp.bfloat16), other[rr], preferred_element_type=jnp.float32)
            igrad_out[...] = (igrad[...] * scale).astype(jnp.bfloat16)
            total = jnp.sum(losses[...].T, axis=0, keepdims=True)
            loss_out[...] = total / ((ROUNDS + 1) * rows)

    for j in range(CHUNKS + 1):
        if j < CHUNKS:
            for rr in range(ROUNDS):
                c[j][rr].wait_recv()
            d[j].start()
        if j >= 1:
            finish(j - 1)
    tgrad_out[...] = (tgrad[...] * scale).astype(jnp.bfloat16)
    for j in range(CHUNKS):
        for sent in (a[j], b[j], c[j][0], c[j][1], d[j]):
            sent.wait_send()


def whole_step(variant, scale, taken, images, texts):
    rows, width = images.shape
    part = rows // PARTS
    vmem = pl.BlockSpec(memory_space=pltpu.VMEM)
    both = pltpu.VMEM((CHUNKS, ROUNDS, part, width), jnp.bfloat16)
    total = pltpu.VMEM((rows, width), jnp.float32)
    far_bits = (FAR, NEAR) if variant else (FAR,)
    return pl.pallas_call(
        functools.partial(kernel, far_bits, scale),
        out_shape=(
            jax.ShapeDtypeStruct((1, rows), jnp.float32),
            jax.ShapeDtypeStruct((rows, width), jnp.bfloat16),
            jax.ShapeDtypeStruct((rows, width), jnp.bfloat16),
        ),
        in_specs=[pl.BlockSpec(memory_space=pltpu.SMEM), vmem, vmem],
        out_specs=(vmem, vmem, vmem),
        scratch_shapes=[
            pltpu.VMEM((CHUNKS, part, width), jnp.bfloat16), both, both, both, both, both,
            pltpu.VMEM((ROUNDS, rows, width), jnp.bfloat16), pltpu.VMEM((rows, rows), jnp.float32), total, total,
            pltpu.SemaphoreType.DMA((2, CHUNKS)), pltpu.SemaphoreType.DMA((2, CHUNKS)),
            pltpu.SemaphoreType.DMA((2, CHUNKS, ROUNDS)), pltpu.SemaphoreType.DMA((2, CHUNKS)),
        ],
        compiler_params=pltpu.CompilerParams(
            collective_id=variant, has_side_effects=True, vmem_limit_bytes=48 * 2**20
        ),
        cost_estimate=pl.CostEstimate(flops=22 * rows * rows * width, bytes_accessed=8 * rows * width, transcendentals=0),
    )(taken, images, texts)


def kernel_shards(images, texts, plan):
    rows, width = images.shape
    scale = TEMPER / width**0.5
    flipped = jnp.bitwise_xor(plan[:, 0], 0)
    shifts = jnp.arange(3, dtype=jnp.int32)
    taken = jnp.bitwise_and(jnp.right_shift(flipped[:, None], shifts[None, :]), 1).astype(jnp.float32)
    crosses = jnp.bitwise_and(flipped[0], NEAR) != 0
    loss, igrad, tgrad = lax.cond(
        crosses, functools.partial(whole_step, 1, scale), functools.partial(whole_step, 0, scale), taken, images, texts
    )
    return loss.reshape(rows), igrad, tgrad


def tile_coeffs(img, txt, labels, scale):
    z = jnp.dot(img, txt.T, preferred_element_type=jnp.float32) * scale + OFFSET
    loss = jnp.sum(jnp.logaddexp(jnp.float32(0.0), -labels * z), axis=1)
    g = (-labels * jax.nn.sigmoid(-labels * z)).astype(jnp.bfloat16)
    return (loss, g)


def coeffs(img, txt, labels, scale):
    z = jnp.dot(img, txt.T, preferred_element_type=jnp.float32) * scale + OFFSET
    return (-labels * jax.nn.sigmoid(-labels * z)).astype(jnp.bfloat16)


def image_side(g, txt, scale):
    return jnp.dot(g, txt, preferred_element_type=jnp.float32) * scale


def text_side(g, img, scale):
    return (
        lax.dot_general(g, img, (((0,), (0,)), ((), ())), preferred_element_type=jnp.float32)
        * scale
    )


def send_pairs(masks, *blocks):
    devices = range(lax.axis_size("dp"))
    return tuple(
        lax.ppermute(block, "dp", [(source, source ^ mask) for source in devices])
        if mask
        else block
        for block, mask in zip(blocks, masks)
    )


def exchange(images, texts, flips):
    nbits = lax.axis_size("dp").bit_length() - 1
    free = [nbits - 1 - rr for rr in range(ROUNDS)]
    digit_bits = HOP_BITS
    held = (images, texts) * ROUNDS
    low = 0
    while low < max(free):
        widths = [max(0, min(digit_bits, bits - low)) for bits in free]
        last = low + digit_bits >= max(free)
        index, count = jnp.int32(0), 1
        for rr, width in enumerate(widths):
            digit = jnp.bitwise_and(jnp.right_shift(flips[rr], low), 2**width - 1)
            index, count = index + digit * count, count * 2**width
        branches = []
        for branch in range(count):
            masks = []
            for bits, width in zip(free, widths):
                mask = (branch % 2**width) << low
                branch //= 2**width
                masks += [mask + (2**bits if last else 0)] * 2
            branches.append(lambda *blocks, masks=tuple(masks): send_pairs(masks, *blocks))
        held = lax.switch(index, branches, *held)
        low += digit_bits
    return [(held[2 * rr], held[2 * rr + 1]) for rr in range(ROUNDS)]


def hop_shards(images, texts, plan):
    rows_here, width = images.shape
    scale = TEMPER / width**0.5
    position = lax.axis_index("dp")
    flips = [jnp.bitwise_xor(plan[rr, position], position) for rr in range(ROUNDS)]
    eye = jnp.eye(rows_here, dtype=jnp.float32)
    diag_labels = 2.0 * eye - 1.0
    neg_labels = jnp.zeros((rows_here, rows_here), jnp.float32) - 1.0
    theirs = exchange(images, texts, flips)
    loss, g_diag = tile_coeffs(images, texts, diag_labels, scale)
    igrad = image_side(g_diag, texts, scale)
    tgrad = text_side(g_diag, images, scale)
    for other_img, other_txt in theirs:
        l2, g_mine = tile_coeffs(images, other_txt, neg_labels, scale)
        loss = loss + l2
        igrad = igrad + image_side(g_mine, other_txt, scale)
        g_theirs = coeffs(other_img, texts, neg_labels, scale)
        partial = text_side(g_theirs, other_img, scale).astype(jnp.bfloat16)
        tgrad = tgrad + partial.astype(jnp.float32)
    row_loss = loss / ((ROUNDS + 1) * rows_here)
    return (row_loss, igrad.astype(jnp.bfloat16), tgrad.astype(jnp.bfloat16))


def solution(mesh):
    placed = (P("dp", None), P("dp", None), P())
    return jax.shard_map(
        kernel_shards if mesh.shape["dp"] == KERNEL_DEVICES else hop_shards,
        mesh=mesh,
        in_specs=placed,
        out_specs=(P("dp"), P("dp", None), P("dp", None)),
        check_vma=False,
    )
```

profile of v0, /device:TPU:0, one launch (start us, length us, event | category | flops | bytes accessed | tf_op | source)
XLA Modules:
  0.0 78.8 jit_solution(12395636873669735827)
XLA Ops:
  0.6 1.2 %slice.8 = s32[1,1]{1,0:T(1,128)} slice(s32[2,32]{1,0:T(2,128)} %param.7), slice={[0:1], [0:1]} | slice | bytes 8 | tf_op jit(solution)/shard_map/slice | solution.py:176
  2.5 0.0 copy-start
  2.5 0.7 copy-done
  3.2 0.1 slice_reduce_fusion
  3.3 0.1 and_convert_fusion
  3.3 73.3 %conditional.1 = (bf16[256,1152]{1,0:T(8,128)(2,1)S(1)}, bf16[256,1152]{1,0:T(8,128)(2,1)S(1)}, f32[256]{0:T(256)S(1)}) conditional(s32[]{:T(128)} %bitcast.2, (f32[2,3]{1,0:T(2,128)S(1)}, bf16[256,1152]{1,0:T(8,128)(2,1)}, bf16[256,1152]{1,0:T(8,128)(2,1)}) %tuple.18, (f32[2,3]{1,0:T(2,128)S(1)}, bf16[256,1152]{1,0:T(8,128)(2,1)}, ...), branch_computations={%region_0.0_spmd, %region_1.0_spmd} | conditional | flops 1660944384 | bytes 2359320 | solution.py:177
  3.5 73.1 %branch_1_fun.1 = (f32[1,256]{1,0:T(1,128)S(1)}, bf16[256,1152]{1,0:T(8,128)(2,1)S(1)}, bf16[256,1152]{1,0:T(8,128)(2,1)S(1)}) custom-call(f32[2,3]{1,0:T(2,128)S(1)} %get-tuple-element.25.taken, bf16[256,1152]{1,0:T(8,128)(2,1)} %get-tuple-element.26.img, bf16[256,1152]{1,0:T(8,128)(2,1)} %get-tuple-element.27.txt), custom_call_target="tpu_custom_call" | custom-call | flops 1660944384 | bytes 2359296 | tf_op jit(solution)/shard_map/cond/branch_1_fun/pallas_call | solution.py:148
  76.6 0.6 copy.15
  77.2 0.8 %copy.16 = bf16[256,1152]{1,0:T(8,128)(2,1)} copy(bf16[256,1152]{1,0:T(8,128)(2,1)S(1)} %get-tuple-element.50) | data formatting | bytes 1179648
  78.0 0.8 %copy.17 = bf16[256,1152]{1,0:T(8,128)(2,1)} copy(bf16[256,1152]{1,0:T(8,128)(2,1)S(1)} %get-tuple-element.51) | data formatting | bytes 1179648
Async XLA Ops:
  2.5 0.7 copy-start
where the time goes:
time: 79 us; the launch traced here: 78.8 us
  Pallas kernels  73.1 us (93%)
  local copies, waits for them, and re-layouts  4.17 us (5%)
  between operations  1.3 us (2%)
    pallas_call x1, Pallas kernels, whole_step(): pl.pallas_call(functools.partial(kernel, far_bits, scale), out_shape=(jax...  73.1 us
    unnamed x5, local copies, waits for them, and re-layouts  2.87 us

commit v1 on v0

--- a/solution.py
+++ b/solution.py
@@ -15,6 +15,7 @@
 CORE, FIRST, SECOND, NEAR, FAR = 1, 2, 4, 8, 16
 PARTS = 4
 CHUNKS = 2 * PARTS
+Z_FIRST = 2
 HOP_BITS = 2
 
 
@@ -43,9 +44,9 @@
 
 
 def kernel(
-    far_bits, scale, taken, img, txt, loss_out, igrad_out, tgrad_out,
-    a_recv, b_send, b_recv, c_send, c_recv, d_recv, other, losses, igrad, tgrad,
-    a_sems, b_sems, c_sems, d_sems,
+    far_bits, scale, plan, img, txt, loss_out, igrad_out, tgrad_out,
+    a_recv, b_send, b_recv, c_send, c_recv, d_recv, e_recv, f_send, f_recv, g_send, other, losses, igrad, tgrad,
+    a_sems, b_sems, c_sems, d_sems, e_sems, f_sems,
 ):
     me = lax.axis_index("dp")
     core, first, second, near = (flip(me, bit) for bit in (CORE, FIRST, SECOND, NEAR))
@@ -54,6 +55,10 @@
         far = flip(far, bit)
     rows = img.shape[0]
     part = rows // PARTS
+    taken = [
+        [jnp.bitwise_and(lax.shift_right_logical(plan[rr, 0], bit), 1).astype(jnp.float32) for bit in range(3)]
+        for rr in range(ROUNDS)
+    ]
 
     barrier = pltpu.get_barrier_semaphore()
     for device in (core, first, second, near, far):
@@ -69,15 +74,22 @@
     def own(j):
         return (txt if j < PARTS else img).at[pl.ds((j % PARTS) * part, part)]
 
+    plane_first, z_first = range(Z_FIRST, CHUNKS), range(Z_FIRST)
     order = [(first, second) if j % 2 == 0 else (second, first) for j in range(CHUNKS)]
     bits = [(1, 2) if j % 2 == 0 else (2, 1) for j in range(CHUNKS)]
-    a = [copy(own(j), a_recv.at[j], a_sems, (j,), order[j][0]) for j in range(CHUNKS)]
-    b = [copy(b_send.at[j], b_recv.at[j], b_sems, (j,), order[j][1]) for j in range(CHUNKS)]
+    a = {j: copy(own(j), a_recv.at[j], a_sems, (j,), order[j][0]) for j in plane_first}
+    b = {j: copy(b_send.at[j], b_recv.at[j], b_sems, (j,), order[j][1]) for j in plane_first}
     c = [
-        [copy(c_send.at[j, rr], c_recv.at[j, rr], c_sems, (j, rr), (far, near)[rr]) for rr in range(ROUNDS)]
+        [
+            copy(own(j) if j < Z_FIRST else c_send.at[j, rr], c_recv.at[j, rr], c_sems, (j, rr), (far, near)[rr])
+            for rr in range(ROUNDS)
+        ]
         for j in range(CHUNKS)
     ]
-    d = [copy(c_recv.at[j], d_recv.at[j], d_sems, (j,), core) for j in range(CHUNKS)]
+    e = {j: copy(c_recv.at[j], e_recv.at[j], e_sems, (j,), order[j][0]) for j in z_first}
+    f = {j: copy(f_send.at[j], f_recv.at[j], f_sems, (j,), order[j][1]) for j in z_first}
+    landed = [g_send.at[j] if j < Z_FIRST else c_recv.at[j] for j in range(CHUNKS)]
+    d = [copy(landed[j], d_recv.at[j], d_sems, (j,), core) for j in range(CHUNKS)]
 
     def diagonal():
         z = logits(img[...], txt[...], scale)
@@ -89,60 +101,86 @@
         igrad[...] = jnp.dot(g, txt[...], preferred_element_type=jnp.float32)
         tgrad[...] = over_rows(g, img[...])
 
-    a[0].start()
-    a[1].start()
-    for j in range(CHUNKS + 1):
+    def along_z(j):
+        for rr in range(ROUNDS):
+            c[j][rr].start()
+
+    def after_z(j):
+        for rr in range(ROUNDS):
+            c[j][rr].wait_recv()
+
+    for j in z_first:
+        along_z(j)
+    for j in plane_first[:2]:
+        a[j].start()
+    diagonal()
+    for j in range(Z_FIRST, CHUNKS + 1):
         if j < CHUNKS:
             a[j].wait_recv()
             for rr in range(ROUNDS):
-                b_send[j, rr] = pick(own(j)[...], a_recv[j], taken[rr, bits[j][0]])
+                b_send[j, rr] = pick(own(j)[...], a_recv[j], taken[rr][bits[j][0]])
             b[j].start()
             if j + 2 < CHUNKS:
                 a[j + 2].start()
-        if j >= 1:
+        if j > Z_FIRST:
             b[j - 1].wait_recv()
             for rr in range(ROUNDS):
-                c_send[j - 1, rr] = pick(b_send[j - 1, rr], b_recv[j - 1, rr], taken[rr, bits[j - 1][1]])
-                c[j - 1][rr].start()
-        if j == 3:
-            diagonal()
-
-    def finish(j):
+                c_send[j - 1, rr] = pick(b_send[j - 1, rr], b_recv[j - 1, rr], taken[rr][bits[j - 1][1]])
+            along_z(j - 1)
+        if j == CHUNKS - 3:
+            for k in z_first:
+                after_z(k)
+                e[k].start()
+    for j in z_first:
+        e[j].wait_recv()
+        for rr in range(ROUNDS):
+            f_send[j, rr] = pick(c_recv[j, rr], e_recv[j, rr], taken[rr][bits[j][0]])
+        f[j].start()
+    for j in range(Z_FIRST, PARTS):
+        after_z(j)
+        d[j].start()
+    for j in z_first:
+        f[j].wait_recv()
+        for rr in range(ROUNDS):
+            g_send[j, rr] = pick(f_send[j, rr], f_recv[j, rr], taken[rr][bits[j][1]])
+        d[j].start()
+
+    def arrive(j, rr):
+        return pick(landed[j][rr], d_recv[j, rr], taken[rr][0])
+
+    for j in (*range(Z_FIRST, PARTS), *z_first):
         d[j].wait_recv()
         for rr in range(ROUNDS):
-            arrived = pick(c_recv[j, rr], d_recv[j, rr], taken[rr, 0])
-            if j < PARTS:
-                other[rr, pl.ds(j * part, part)] = arrived
-            else:
-                _, slope = loss_and_slope(logits(arrived, txt[...], scale))
-                tgrad[...] += over_rows(slope.astype(jnp.bfloat16), arrived)
-        if j == PARTS - 1:
-            for rr in range(ROUNDS):
-                loss, slope = loss_and_slope(logits(img[...], other[rr], scale))
-                losses[...] += loss
-                igrad[...] += jnp.dot(slope.astype(jnp.bfloat16), other[rr], preferred_element_type=jnp.float32)
-            igrad_out[...] = (igrad[...] * scale).astype(jnp.bfloat16)
-            total = jnp.sum(losses[...].T, axis=0, keepdims=True)
-            loss_out[...] = total / ((ROUNDS + 1) * rows)
-
-    for j in range(CHUNKS + 1):
-        if j < CHUNKS:
-            for rr in range(ROUNDS):
-                c[j][rr].wait_recv()
-            d[j].start()
-        if j >= 1:
-            finish(j - 1)
+            other[rr, pl.ds(j * part, part)] = arrive(j, rr)
+    after_z(PARTS)
+    d[PARTS].start()
+    for rr in range(ROUNDS):
+        loss, slope = loss_and_slope(logits(img[...], other[rr], scale))
+        losses[...] += loss
+        igrad[...] += jnp.dot(slope.astype(jnp.bfloat16), other[rr], preferred_element_type=jnp.float32)
+    igrad_out[...] = (igrad[...] * scale).astype(jnp.bfloat16)
+    loss_out[...] = jnp.sum(losses[...].T, axis=0, keepdims=True) / ((ROUNDS + 1) * rows)
+    for j in range(PARTS, CHUNKS):
+        if j + 1 < CHUNKS:
+            after_z(j + 1)
+            d[j + 1].start()
+        d[j].wait_recv()
+        for rr in range(ROUNDS):
+            arrived = arrive(j, rr)
+            _, slope = loss_and_slope(logits(arrived, txt[...], scale))
+            tgrad[...] += over_rows(slope.astype(jnp.bfloat16), arrived)
     tgrad_out[...] = (tgrad[...] * scale).astype(jnp.bfloat16)
     for j in range(CHUNKS):
-        for sent in (a[j], b[j], c[j][0], c[j][1], d[j]):
+        for sent in (*((e[j], f[j]) if j < Z_FIRST else (a[j], b[j])), *c[j], d[j]):
             sent.wait_send()
 
 
-def whole_step(variant, scale, taken, images, texts):
+def whole_step(variant, scale, plan, images, texts):
     rows, width = images.shape
     part = rows // PARTS
     vmem = pl.BlockSpec(memory_space=pltpu.VMEM)
     both = pltpu.VMEM((CHUNKS, ROUNDS, part, width), jnp.bfloat16)
+    early = pltpu.VMEM((Z_FIRST, ROUNDS, part, width), jnp.bfloat16)
     total = pltpu.VMEM((rows, width), jnp.float32)
     far_bits = (FAR, NEAR) if variant else (FAR,)
     return pl.pallas_call(
@@ -155,27 +193,25 @@
         in_specs=[pl.BlockSpec(memory_space=pltpu.SMEM), vmem, vmem],
         out_specs=(vmem, vmem, vmem),
         scratch_shapes=[
-            pltpu.VMEM((CHUNKS, part, width), jnp.bfloat16), both, both, both, both, both,
+            pltpu.VMEM((CHUNKS, part, width), jnp.bfloat16), both, both, both, both, both, early, early, early, early,
             pltpu.VMEM((ROUNDS, rows, width), jnp.bfloat16), pltpu.VMEM((rows, rows), jnp.float32), total, total,
             pltpu.SemaphoreType.DMA((2, CHUNKS)), pltpu.SemaphoreType.DMA((2, CHUNKS)),
             pltpu.SemaphoreType.DMA((2, CHUNKS, ROUNDS)), pltpu.SemaphoreType.DMA((2, CHUNKS)),
+            pltpu.SemaphoreType.DMA((2, Z_FIRST)), pltpu.SemaphoreType.DMA((2, Z_FIRST)),
         ],
         compiler_params=pltpu.CompilerParams(
             collective_id=variant, has_side_effects=True, vmem_limit_bytes=48 * 2**20
         ),
         cost_estimate=pl.CostEstimate(flops=22 * rows * rows * width, bytes_accessed=8 * rows * width, transcendentals=0),
-    )(taken, images, texts)
+    )(plan, images, texts)
 
 
 def kernel_shards(images, texts, plan):
     rows, width = images.shape
     scale = TEMPER / width**0.5
-    flipped = jnp.bitwise_xor(plan[:, 0], 0)
-    shifts = jnp.arange(3, dtype=jnp.int32)
-    taken = jnp.bitwise_and(jnp.right_shift(flipped[:, None], shifts[None, :]), 1).astype(jnp.float32)
-    crosses = jnp.bitwise_and(flipped[0], NEAR) != 0
+    crosses = jnp.bitwise_and(plan[0, 0], NEAR) != 0
     loss, igrad, tgrad = lax.cond(
-        crosses, functools.partial(whole_step, 1, scale), functools.partial(whole_step, 0, scale), taken, images, texts
+        crosses, functools.partial(whole_step, 1, scale), functools.partial(whole_step, 0, scale), plan, images, texts
     )
     return loss.reshape(rows), igrad, tgrad
 

time: 79 us -> 67.3 us (0.85)
  Pallas kernels: 73.1 us -> 61.6 us
    pallas_call x1, Pallas kernels: 73.1 us -> 61.6 us  [whole_step(): pl.pallas_call(functools.partial(kernel, far_bits, scale), out_shape=(jax...]
where the time goes in v1:
time: 67.3 us; the launch traced here: 67.1 us
  Pallas kernels  61.6 us (92%)
  local copies, waits for them, and re-layouts  4.06 us (6%)
  between operations  1.3 us (2%)
    pallas_call x1, Pallas kernels, whole_step(): pl.pallas_call(functools.partial(kernel, far_bits, scale), out_shape=(jax...  61.6 us
    unnamed x5, local copies, waits for them, and re-layouts  2.87 us

profile of v1, /device:TPU:0, one launch (start us, length us, event | category | flops | bytes accessed | tf_op | source)
XLA Modules:
  0.0 67.1 jit_solution(11237361448846580484)
XLA Ops:
  0.6 1.2 %slice.3 = s32[1,1]{1,0:T(1,128)} slice(s32[2,32]{1,0:T(2,128)} %param.7), slice={[0:1], [0:1]} | slice | bytes 8 | tf_op jit(solution)/shard_map/slice | solution.py:212
  2.5 0.0 copy-start
  2.5 0.7 copy-done
  3.2 61.7 %conditional.1 = (bf16[256,1152]{1,0:T(8,128)(2,1)S(1)}, bf16[256,1152]{1,0:T(8,128)(2,1)S(1)}, f32[256]{0:T(256)S(1)}) conditional(s32[]{:T(128)} %bitcast.2, (s32[2,32]{1,0:T(2,128)S(1)}, bf16[256,1152]{1,0:T(8,128)(2,1)}, bf16[256,1152]{1,0:T(8,128)(2,1)}) %tuple.24, (s32[2,32]{1,0:T(2,128)S(1)}, bf16[256,1152]{1,0:T(8,128)(2,1)}, ...), branch_computations={%region_0.0_spmd, %region_1.0_spmd} | conditional | flops 1660944384 | bytes 2359320 | solution.py:213
  3.2 61.6 %branch_0_fun.1 = (f32[1,256]{1,0:T(1,128)S(1)}, bf16[256,1152]{1,0:T(8,128)(2,1)S(1)}, bf16[256,1152]{1,0:T(8,128)(2,1)S(1)}) custom-call(s32[2,32]{1,0:T(2,128)S(1)} %get-tuple-element.19.plan, bf16[256,1152]{1,0:T(8,128)(2,1)} %get-tuple-element.20.img, bf16[256,1152]{1,0:T(8,128)(2,1)} %get-tuple-element.21.txt), custom_call_target="tpu_custom_call" | custom-call | flops 1660944384 | bytes 2359296 | tf_op jit(solution)/shard_map/cond/branch_0_fun/pallas_call | solution.py:186
  64.9 0.6 copy.15
  65.5 0.8 %copy.16 = bf16[256,1152]{1,0:T(8,128)(2,1)} copy(bf16[256,1152]{1,0:T(8,128)(2,1)S(1)} %get-tuple-element.50) | data formatting | bytes 1179648
  66.3 0.8 %copy.17 = bf16[256,1152]{1,0:T(8,128)(2,1)} copy(bf16[256,1152]{1,0:T(8,128)(2,1)S(1)} %get-tuple-element.51) | data formatting | bytes 1179648
Async XLA Ops:
  2.5 0.7 %copy-start = (s32[2,32]{1,0:T(2,128)S(1)}, s32[2,32]{1,0:T(2,128)}, u32[]{:S(2)}) copy-start(s32[2,32]{1,0:T(2,128)} %param.7) | copy-start | bytes 772

commit v2 on v1

--- a/solution.py
+++ b/solution.py
@@ -206,6 +206,25 @@
     )(plan, images, texts)
 
 
+def hand_over(*arrays):
+    def copies(*refs):
+        n = len(arrays)
+        moves = [pltpu.make_async_copy(refs[k], refs[n + k], refs[2 * n].at[k]) for k in range(n)]
+        for move in moves:
+            move.start()
+        for move in moves:
+            move.wait()
+
+    anywhere = pl.BlockSpec(memory_space=pl.ANY)
+    return pl.pallas_call(
+        copies,
+        out_shape=[jax.ShapeDtypeStruct(array.shape, array.dtype) for array in arrays],
+        in_specs=[anywhere] * len(arrays),
+        out_specs=[anywhere] * len(arrays),
+        scratch_shapes=[pltpu.SemaphoreType.DMA((len(arrays),))],
+    )(*arrays)
+
+
 def kernel_shards(images, texts, plan):
     rows, width = images.shape
     scale = TEMPER / width**0.5
@@ -213,6 +232,7 @@
     loss, igrad, tgrad = lax.cond(
         crosses, functools.partial(whole_step, 1, scale), functools.partial(whole_step, 0, scale), plan, images, texts
     )
+    loss, igrad, tgrad = hand_over(loss, igrad, tgrad)
     return loss.reshape(rows), igrad, tgrad
 
 

time: 67.3 us -> 65.8 us (0.978)
  local copies, waits for them, and re-layouts: 4.06 us -> 1.87 us
    unnamed x5 -> x2, local copies, waits for them, and re-layouts: 2.87 us -> 0.67 us
    pallas_call x0 -> x1, Pallas kernels: none -> 1.04 us  [hand_over(): pl.pallas_call(copies, out_shape=[jax.ShapeDtypeStruct(array.shape, array...]
    pallas_call x1, Pallas kernels: 61.6 us -> 60.7 us  [whole_step(): pl.pallas_call(functools.partial(kernel, far_bits, scale), out_shape=(jax...]
where the time goes in v2:
time: 65.8 us; the launch traced here: 65.1 us
  Pallas kernels  61.8 us (94%)
  local copies, waits for them, and re-layouts  1.87 us (3%)
  between operations  1.46 us (2%)
    pallas_call x1, Pallas kernels, whole_step(): pl.pallas_call(functools.partial(kernel, far_bits, scale), out_shape=(jax...  60.7 us

profile of v2, /device:TPU:0, one launch (start us, length us, event | category | flops | bytes accessed | tf_op | source)
XLA Modules:
  0.0 65.1 jit_solution(7162802864914486711)
XLA Ops:
  0.6 1.2 %slice.3 = s32[1,1]{1,0:T(1,128)} slice(s32[2,32]{1,0:T(2,128)} %param.7), slice={[0:1], [0:1]} | slice | bytes 8 | tf_op jit(solution)/shard_map/slice | solution.py:231
  2.5 0.0 copy-start
  2.5 0.7 %copy-done = s32[2,32]{1,0:T(2,128)S(1)} copy-done((s32[2,32]{1,0:T(2,128)S(1)}, s32[2,32]{1,0:T(2,128)}, u32[]{:S(2)}) %copy-start) | copy-done | bytes 280
  3.2 60.7 %conditional.1 = ((f32[1,256]{1,0:T(1,128)S(1)}, bf16[256,1152]{1,0:T(8,128)(2,1)S(1)}, bf16[256,1152]{1,0:T(8,128)(2,1)S(1)})) conditional(s32[]{:T(128)} %bitcast, (s32[2,32]{1,0:T(2,128)S(1)}, bf16[256,1152]{1,0:T(8,128)(2,1)}, bf16[256,1152]{1,0:T(8,128)(2,1)}) %tuple.20, (s32[2,32]{1,0:T(2,128)S(1)}, bf16[256,1152]{1,0:T(8,128)(2,1)}, ...), branch_computations={%region_0.0_spmd, %region_1.0_spmd} | conditional | flops 1660944384 | bytes 2359304 | solution.py:232
  3.2 60.7 %branch_1_fun.1 = (f32[1,256]{1,0:T(1,128)S(1)}, bf16[256,1152]{1,0:T(8,128)(2,1)S(1)}, bf16[256,1152]{1,0:T(8,128)(2,1)S(1)}) custom-call(s32[2,32]{1,0:T(2,128)S(1)} %get-tuple-element.15.plan, bf16[256,1152]{1,0:T(8,128)(2,1)} %get-tuple-element.16.img, bf16[256,1152]{1,0:T(8,128)(2,1)} %get-tuple-element.17.txt), custom_call_target="tpu_custom_call" | custom-call | flops 1660944384 | bytes 2359296 | tf_op jit(solution)/shard_map/cond/branch_1_fun/pallas_call | solution.py:186
  63.9 1.0 %shard_map.58 = (f32[1,256]{1,0:T(1,128)}, bf16[256,1152]{1,0:T(8,128)(2,1)}, bf16[256,1152]{1,0:T(8,128)(2,1)}) custom-call(f32[1,256]{1,0:T(1,128)S(1)} %get-tuple-element.27.refs_0_, bf16[256,1152]{1,0:T(8,128)(2,1)S(1)} %get-tuple-element.28.refs_1_, bf16[256,1152]{1,0:T(8,128)(2,1)S(1)} %get-tuple-element.29.refs_2_), custom_call_target="tpu_custom_call" | custom-call | tf_op jit(solution)/shard_map/pallas_call | solution.py:219
Async XLA Ops:
  2.5 0.7 %copy-start = (s32[2,32]{1,0:T(2,128)S(1)}, s32[2,32]{1,0:T(2,128)}, u32[]{:S(2)}) copy-start(s32[2,32]{1,0:T(2,128)} %param.7) | copy-start | bytes 772

commit v3 on v2

--- a/solution.py
+++ b/solution.py
@@ -165,10 +165,9 @@
             after_z(j + 1)
             d[j + 1].start()
         d[j].wait_recv()
-        for rr in range(ROUNDS):
-            arrived = arrive(j, rr)
-            _, slope = loss_and_slope(logits(arrived, txt[...], scale))
-            tgrad[...] += over_rows(slope.astype(jnp.bfloat16), arrived)
+        arrived = jnp.concatenate([arrive(j, rr) for rr in range(ROUNDS)], axis=0)
+        _, slope = loss_and_slope(logits(arrived, txt[...], scale))
+        tgrad[...] += over_rows(slope.astype(jnp.bfloat16), arrived)
     tgrad_out[...] = (tgrad[...] * scale).astype(jnp.bfloat16)
     for j in range(CHUNKS):
         for sent in (*((e[j], f[j]) if j < Z_FIRST else (a[j], b[j])), *c[j], d[j]):

time: 65.8 us -> 65.1 us (0.989)
  no operation moved by 1% of the time
where the time goes in v3:
time: 65.1 us; the launch traced here: 65 us
  Pallas kernels  61.5 us (94%)
  local copies, waits for them, and re-layouts  1.87 us (3%)
  between operations  1.46 us (2%)
    pallas_call x1, Pallas kernels, whole_step(): pl.pallas_call(functools.partial(kernel, far_bits, scale), out_shape=(jax...  60.4 us

profile of v3, /device:TPU:0, one launch (start us, length us, event | category | flops | bytes accessed | tf_op | source)
XLA Modules:
  0.0 65.0 jit_solution(4133758705203603282)
XLA Ops:
  0.6 1.2 %slice.3 = s32[1,1]{1,0:T(1,128)} slice(s32[2,32]{1,0:T(2,128)} %param.7), slice={[0:1], [0:1]} | slice | bytes 8 | tf_op jit(solution)/shard_map/slice | solution.py:230
  2.5 0.0 copy-start
  2.5 0.7 %copy-done = s32[2,32]{1,0:T(2,128)S(1)} copy-done((s32[2,32]{1,0:T(2,128)S(1)}, s32[2,32]{1,0:T(2,128)}, u32[]{:S(2)}) %copy-start) | copy-done | bytes 280
  3.2 60.6 %conditional.1 = ((f32[1,256]{1,0:T(1,128)S(1)}, bf16[256,1152]{1,0:T(8,128)(2,1)S(1)}, bf16[256,1152]{1,0:T(8,128)(2,1)S(1)})) conditional(s32[]{:T(128)} %bitcast, (s32[2,32]{1,0:T(2,128)S(1)}, bf16[256,1152]{1,0:T(8,128)(2,1)}, bf16[256,1152]{1,0:T(8,128)(2,1)}) %tuple.20, (s32[2,32]{1,0:T(2,128)S(1)}, bf16[256,1152]{1,0:T(8,128)(2,1)}, ...), branch_computations={%region_0.0_spmd, %region_1.0_spmd} | conditional | flops 1660944384 | bytes 2359304 | solution.py:231
  3.2 60.4 %branch_0_fun.1 = (f32[1,256]{1,0:T(1,128)S(1)}, bf16[256,1152]{1,0:T(8,128)(2,1)S(1)}, bf16[256,1152]{1,0:T(8,128)(2,1)S(1)}) custom-call(s32[2,32]{1,0:T(2,128)S(1)} %get-tuple-element.12.plan, bf16[256,1152]{1,0:T(8,128)(2,1)} %get-tuple-element.13.img, bf16[256,1152]{1,0:T(8,128)(2,1)} %get-tuple-element.14.txt), custom_call_target="tpu_custom_call" | custom-call | flops 1660944384 | bytes 2359296 | tf_op jit(solution)/shard_map/cond/branch_0_fun/pallas_call | solution.py:185
  63.8 1.0 %shard_map.58 = (f32[1,256]{1,0:T(1,128)}, bf16[256,1152]{1,0:T(8,128)(2,1)}, bf16[256,1152]{1,0:T(8,128)(2,1)}) custom-call(f32[1,256]{1,0:T(1,128)S(1)} %get-tuple-element.27.refs_0_, bf16[256,1152]{1,0:T(8,128)(2,1)S(1)} %get-tuple-element.28.refs_1_, bf16[256,1152]{1,0:T(8,128)(2,1)S(1)} %get-tuple-element.29.refs_2_), custom_call_target="tpu_custom_call" | custom-call | tf_op jit(solution)/shard_map/pallas_call | solution.py:218
Async XLA Ops:
  2.5 0.7 %copy-start = (s32[2,32]{1,0:T(2,128)S(1)}, s32[2,32]{1,0:T(2,128)}, u32[]{:S(2)}) copy-start(s32[2,32]{1,0:T(2,128)} %param.7) | copy-start | bytes 772
